TPU v7x, 32 devices: a whole 2x2x4 slice. The times are simulated.
32 devices in a mesh: series: 16 (over z, y, core), tm: 2 (over x).
Axes of the slice: x: 2, y: 2, z: 4, core: 2. Of those that a mesh axis runs over, the one named last changes fastest.
Arguments:
- data: float32 [16384, 2048], P('series', 'tm'), may hold values from -36 to 36, as said below
- sparse: float32 [16384, 2048], P('series', 'tm'), may hold values from -4 to 4
- omega: bfloat16 [2048, 256], P('tm'), may hold values from -0.125 to 0.125
- svt_scale: float32 [1], replicated, may hold values from 0.6 to 1.2
- sparse_threshold: float32 [1], replicated, may hold values from 0.3 to 1.5
Outputs:
- low_rank: float32 [16384, 2048], P('series', 'tm')
- sparse_new: float32 [16384, 2048], P('series', 'tm')
Inputs may be any that keep to these rules, and one draw needn't show every extreme that they name: `data`: each entry is a series scale times a minute scale times a bounded random value.
All inputs are finite; a program needn't handle non-finite values.
Results may differ from a plain program's by a relative error of at most 0.003.
Values sent between devices are 32-bit elements; how exact they have to be, the bound alone decides.
A program may use at most 64 MiB of HBM per device.

v0:
```python
import jax
import jax.numpy as jnp
from jax import lax
from jax.sharding import PartitionSpec as P

ROOT_STEPS = 12
SIGN_STEPS = 12


def shrink_factor(gram, svt_scale):
    highest = lax.Precision.HIGHEST
    columns = gram.shape[0]
    identity = jnp.eye(columns, dtype=jnp.float32)
    magnitude = jnp.linalg.norm(gram)
    threshold = svt_scale[0] * jnp.sqrt(jnp.trace(gram) / columns)

    def root_turn(counter, state):
        root_part, inverse_root = state
        middle = 1.5 * identity - 0.5 * jnp.dot(inverse_root, root_part, precision=highest)
        return (
            jnp.dot(root_part, middle, precision=highest),
            jnp.dot(middle, inverse_root, precision=highest),
        )

    root_part, inverse_root = lax.fori_loop(0, ROOT_STEPS, root_turn, (gram / magnitude, identity))
    root_scale = jnp.sqrt(magnitude)
    shifted = root_scale * root_part - threshold * identity
    signed = shifted / jnp.sqrt(jnp.sum(shifted * shifted) + 1e-06)

    def sign_turn(counter, signed):
        return 1.5 * signed - 0.5 * jnp.dot(
            signed, jnp.dot(signed, signed, precision=highest), precision=highest
        )

    signed = lax.fori_loop(0, SIGN_STEPS, sign_turn, signed)
    damping = identity - threshold / root_scale * inverse_root
    return 0.5 * jnp.dot(identity + signed, damping, precision=highest)


def lower_solve(lower_factor, right_part):
    return lax.linalg.triangular_solve(lower_factor, right_part, left_side=True, lower=True)


def on_device(data, sparse, omega, svt_scale, sparse_threshold):
    highest = lax.Precision.HIGHEST
    residual = data - sparse
    rounded = residual.astype(jnp.bfloat16)
    sketch_terms = jnp.dot(rounded, omega, preferred_element_type=jnp.float32)
    sketch = lax.psum(sketch_terms, "tm")
    sketch_t = sketch.T
    gram_first = lax.psum(jnp.dot(sketch_t, sketch, precision=highest), "series")
    basis_t = lower_solve(jnp.linalg.cholesky(gram_first), sketch_t)
    projection = lax.psum(jnp.dot(basis_t, residual, precision=highest), "series")
    gram = lax.psum(jnp.dot(projection, projection.T, precision=highest), "tm")
    factor = shrink_factor(gram, svt_scale)
    low_rank = jnp.dot(basis_t.T, jnp.dot(factor, projection, precision=highest), precision=highest)
    gap = data - low_rank
    sparse_new = jnp.sign(gap) * jnp.maximum(jnp.abs(gap) - sparse_threshold[0], 0.0)
    return (low_rank, sparse_new)


def solution(mesh):
    placed = (P("series", "tm"), P("series", "tm"), P("tm", None), P(), P())
    return jax.shard_map(
        on_device,
        mesh=mesh,
        in_specs=placed,
        out_specs=(P("series", "tm"), P("series", "tm")),
        check_vma=False,
    )
```

profile of v0, /device:TPU:0, one launch (start us, length us, event | category | flops | bytes accessed | tf_op | source)
XLA Modules:
  0.0 398.1 jit_solution(8194029316137840012)
XLA Ops:
  7.2 4.4 %sub.24 = f32[1024,1024]{1,0:T(8,128)S(1)} subtract(f32[1024,1024]{1,0:T(8,128)} %param.9, f32[1024,1024]{1,0:T(8,128)} %param.10) | non-fusion elementwise | flops 1048576 | bytes 12582912 | tf_op jit(solution)/shard_map/sub | solution.py:46
  11.7 2.0 copy-done.1
  13.7 1.7 fusion.5
  15.4 42.9 %all-reduce.6.cloned.1.call-done = f32[1024,256]{1,0:T(8,128)} async-done(((f32[1024,256]{1,0:T(8,128)}), f32[1024,256]{1,0:T(8,128)}) %all-reduce.6.cloned.1.call-update) | async-done | bytes 1048592 | tf_op jit(solution)/shard_map/psum | solution.py:49
  58.3 4.1 %fusion.29 = f32[256,256]{0,1:T(8,128)} fusion(f32[1024,256]{1,0:T(8,128)} %all-reduce.6.cloned.1.call-done), kind=kOutput, calls=%fused_computation.59 | convolution fusion | flops 805306368 | bytes 1310720 | tf_op jit(solution)/shard_map/dot_general | solution.py:51
  62.7 88.7 %all-reduce.8.cloned.1.call-done = f32[256,256]{0,1:T(8,128)} async-done(((f32[256,256]{0,1:T(8,128)}), f32[256,256]{0,1:T(8,128)}) %all-reduce.8.cloned.1.call-update) | async-done | bytes 262160 | tf_op jit(solution)/shard_map/psum | solution.py:51
  151.4 1.1 copy.8
  152.5 1.0 fusion.11
  153.5 11.7 %cholesky.50 = f32[128,128]{1,0:T(8,128)S(1)} custom-call(f32[128,128]{1,0:T(8,128)S(1)} %cholesky.118), custom_call_target="Cholesky" | custom-call | tf_op jit(solution)/shard_map/jit(cholesky)/cholesky | solution.py:52
  165.2 9.8 %custom-call.14 = f32[1,128,128]{1,2,0:T(8,128)S(1)} custom-call(f32[1,128,128]{2,1,0:T(8,128)S(1)} %get-tuple-element.86), custom_call_target="InvertDiagBlocksLowerTriangular" | custom-call | tf_op jit(solution)/shard_map/jit(cholesky)/cholesky | solution.py:52
  175.6 11.7 %cholesky.105 = f32[128,128]{1,0:T(8,128)S(1)} custom-call(f32[128,128]{1,0:T(8,128)S(1)} %convolution_subtract_fusion.1), custom_call_target="Cholesky" | custom-call | tf_op jit(solution)/shard_map/jit(cholesky)/cholesky | solution.py:52
  187.3 0.7 compare_reduce_fusion
  189.5 4.3 %while.25 = (s32[]{:T(128)}, f32[256,256]{1,0:T(8,128)S(1)}, s32[2,2]{1,0:T(2,128)S(1)}, f32[2,128,128]{2,1,0:T(8,128)S(1)}, s32[]{:T(128)}) while((s32[]{:T(128)}, f32[256,256]{1,0:T(8,128)S(1)}, s32[2,2]{1,0:T(2,128)S(1)}, f32[2,128,128]{2,1,0:T(8,128)S(1)}, s32[]{:T(128)}) %tuple.60), condition=%wide.while_cond, body=%wide.while_body.sunk | while | flops 2 | bytes 131189 | solution.py:41
  190.3 1.4 bitcast_dynamic-update-slice_fusion.2
  192.3 1.4 bitcast_dynamic-update-slice_fusion.2
  193.8 19.7 %custom-call.15 = f32[2,128,128]{1,2,0:T(8,128)S(1)} custom-call(f32[2,128,128]{2,1,0:T(8,128)S(1)} %get-tuple-element.47), custom_call_target="InvertDiagBlocksLowerTriangular" | custom-call | tf_op jit(solution)/shard_map/triangular_solve | solution.py:41
  213.4 0.6 fusion.9
  214.1 1.0 convolution_subtract_fusion
  215.1 0.6 fusion.20
  215.7 6.8 %fusion.8 = f32[256,1024]{1,0:T(8,128)} fusion(f32[1024,1024]{1,0:T(8,128)} %copy-done.1, f32[128,1024]{1,0:T(8,128)S(1)} %fusion.20, f32[128,1024]{1,0:T(8,128)S(1)} %fusion.9), kind=kOutput, calls=%fused_computation.18 | convolution fusion | flops 3221487616 | bytes 6291456 | tf_op jit(solution)/shard_map/dot_general | solution.py:53
  222.6 93.8 %all-reduce.10.cloned.1.call-done = f32[256,1024]{1,0:T(8,128)} async-done(((f32[256,1024]{1,0:T(8,128)}), f32[256,1024]{1,0:T(8,128)}) %all-reduce.10.cloned.1.call-update) | async-done | bytes 1048592 | tf_op jit(solution)/shard_map/psum | solution.py:53
  316.4 3.3 fusion.30
  321.0 21.3 %all-reduce.12.cloned.1.call-done = f32[256,256]{1,0:T(8,128)} async-done(((f32[256,256]{1,0:T(8,128)}), f32[256,256]{1,0:T(8,128)}) %all-reduce.12.cloned.1.call-update) | async-done | bytes 262160 | tf_op jit(solution)/shard_map/psum | solution.py:54
  342.3 1.6 select_reduce_fusion
  345.3 1.0 broadcast_divide_fusion
  346.4 18.0 %while.26 = (s32[]{:T(128)}, f32[256,256]{0,1:T(8,128)S(1)}, f32[256,256]{1,0:T(8,128)S(1)}, s32[]{:T(128)}) while((s32[]{:T(128)}, f32[256,256]{0,1:T(8,128)S(1)}, f32[256,256]{1,0:T(8,128)S(1)}, s32[]{:T(128)}) %tuple.63), condition=%wide.region_10.11_spmd.clone, body=%wide.region_9.10_spmd.clone.sunk | while | flops 604241920 | bytes 3407925 | solution.py:25
  349.0 0.6 convolution_bitcast_fusion.2
  350.5 0.6 convolution_bitcast_fusion.2
  353.5 0.6 convolution_bitcast_fusion.2
  355.0 0.6 convolution_bitcast_fusion.2
  359.4 0.6 convolution_bitcast_fusion.2
  363.8 0.6 convolution_bitcast_fusion.2
  364.6 0.7 multiply_reduce_fusion
  366.2 15.0 %while.24 = (s32[]{:T(128)}, f32[256,256]{0,1:T(8,128)S(1)}, s32[]{:T(128)}) while((s32[]{:T(128)}, f32[256,256]{0,1:T(8,128)S(1)}, s32[]{:T(128)}) %tuple.66), condition=%wide.region_14.15_spmd, body=%wide.region_13.14_spmd.sunk | while | flops 402849792 | bytes 1835053 | solution.py:35
  366.8 0.6 fusion.75
  368.1 0.6 fusion.75
  369.3 0.6 fusion.75
  370.6 0.6 fusion.75
  371.8 0.6 fusion.75
  373.1 0.6 fusion.75
  374.3 0.6 fusion.75
  375.6 0.6 fusion.75
  376.8 0.6 fusion.75
  378.1 0.6 fusion.75
  379.3 0.6 fusion.75
  380.6 0.6 fusion.75
  381.8 1.0 fusion.31
  382.8 8.7 %maximum_multiply_fusion = (f32[1024,1024]{1,0:T(8,128)}, f32[1024,1024]{1,0:T(8,128)}) fusion(f32[1024,1024]{1,0:T(8,128)} %param.9, f32[]{:T(128)} %bitcast.84, f32[256,1024]{1,0:T(8,128)S(1)} %fusion.31, f32[128,1024]{1,0:T(8,128)S(1)} %fusion.20, f32[128,1024]{1,0:T(8,128)S(1)} %fusion.9), kind=kOutput, calls=%fused_computation.10 | convolution fusion | flops 3227779072 | bytes 14680068 | tf_op jit(solution)/shard_map/dot_general | solution.py:56
  (114 shorter events, 24.2 us)
Async XLA Ops:
  7.2 6.5 %copy-start = (bf16[1024,256]{1,0:T(8,128)(2,1)S(1)}, bf16[1024,256]{1,0:T(8,128)(2,1)}, u32[]{:S(2)}) copy-start(bf16[1024,256]{1,0:T(8,128)(2,1)} %param.11) | copy-start | bytes 1572868
  7.2 51.1 %all-reduce.6.cloned.1.call-start = ((), (), s32[]{:S(2)}) async-start(), calls=%async_computation | async-start | bytes 2097152 | tf_op jit(solution)/shard_map/psum | solution.py:49
  11.7 2.0 copy-start.1
  15.4 136.0 %all-reduce.8.cloned.1.call-start = ((), (), s32[]{:S(2)}) async-start(), calls=%async_computation.1 | async-start | bytes 524288 | tf_op jit(solution)/shard_map/psum | solution.py:51
  58.3 155.1 %copy-start.3 = (f32[1024,256]{1,0:T(8,128)S(1)}, f32[1024,256]{1,0:T(8,128)}, u32[]{:S(2)}) copy-start(f32[1024,256]{1,0:T(8,128)} %all-reduce.6.cloned.1.call-done) | copy-start | bytes 3145732
  62.5 253.9 %all-reduce.10.cloned.1.call-start = ((), (), s32[]{:S(2)}) async-start(), calls=%async_computation.2 | async-start | bytes 2097152 | tf_op jit(solution)/shard_map/psum | solution.py:53
  222.6 119.7 %all-reduce.12.cloned.1.call-start = ((), (), s32[]{:S(2)}) async-start(), calls=%async_computation.3 | async-start | bytes 524288 | tf_op jit(solution)/shard_map/psum | solution.py:54
  366.2 15.6 %copy-start.2 = (f32[256,1024]{1,0:T(8,128)S(1)}, f32[256,1024]{1,0:T(8,128)}, u32[]{:S(2)}) copy-start(f32[256,1024]{1,0:T(8,128)} %all-reduce.10.cloned.1.call-done) | copy-start | bytes 3145732
Sparse Core Ops, SparseCore 0:
  15.5 42.7 all-reduce.5
  62.7 88.6 all-reduce.7
  222.7 93.6 all-reduce.9
  319.8 22.4 all-reduce.11
where the time goes:
time: 398 us
  waiting for transfers between devices  247 us (62%)
  other arithmetic  62.5 us (16%)
  matrix products  59.8 us (15%)
  between operations  18.7 us (5%)
  local copies, waits for them, and re-layouts  8.45 us (2%)
    psum x1, waiting for transfers between devices, on_device(): lax.psum(jnp.dot(basis_t, residual, precision=highest), 'series')  93.8 us
    psum x1, waiting for transfers between devices, on_device(): lax.psum(jnp.dot(sketch_t, sketch, precision=highest), 'series')  88.7 us
    psum x1, waiting for transfers between devices, on_device(): sketch = lax.psum(sketch_terms, 'tm')  42.9 us
    another operation x6, other arithmetic, on_device(): basis_t = lower_solve(jnp.linalg.cholesky(gram_first), sketch_t)  34 us
    psum x1, waiting for transfers between devices, on_device(): gram = lax.psum(jnp.dot(projection, projection.T, precision=highest), 'tm')  21.3 us
    another operation x3, other arithmetic, lower_solve(): lax.linalg.triangular_solve(lower_factor, right_part, left_side=True, low...  19.7 us
    dot_general x1, matrix products, on_device(): jnp.dot(basis_t.T, jnp.dot(factor, projection, precision=highest), precis...  8.75 us
  transfers between devices with their start and end apart: 4, of which 4 were waited for; matrix products, arithmetic and copies ran while one was open for 0% of the time, Pallas kernels for 0%

commit v1 on v0

v1 whole, which is shorter than its diff:
```python
import functools

import jax
import jax.numpy as jnp
from jax import lax
from jax.experimental import pallas as pl
from jax.experimental.pallas import tpu as pltpu
from jax.sharding import PartitionSpec as P

ROOT_STEPS = 12
SIGN_STEPS = 12
BASIS_STEPS = 60
CHUNKS = 4
F32 = jnp.float32
BF16 = jnp.bfloat16
MESH = pl.DeviceIdType.MESH


def split(x):
    high = x.astype(BF16)
    return high, (x - high.astype(F32)).astype(BF16)


def dot_split(a, b, dims=((1,), (0,))):
    mul = functools.partial(
        lax.dot_general, dimension_numbers=(dims, ((), ())), preferred_element_type=F32
    )
    (ah, al), (bh, bl) = a, b
    return mul(ah, bh) + (mul(ah, bl) + mul(al, bh))


def mm(a, b):
    return dot_split(split(a), split(b))


def halvings(columns, series):
    steps, rows, place, bit = [], columns, 0, 1
    while bit < series:
        sent = rows // 2 if rows >= 16 else rows
        steps.append((bit, rows, sent, place))
        place += sent
        rows = sent
        bit *= 2
    return steps, place


def gather_kernel(
    series, tm, data_hbm, sparse_hbm, omega_ref, sketch_ref, sums_ref, gram_ref,
    data_v, sparse_v, own, arrived, total, halves, gram_own, gram_in,
    load_sem, sk_send, sk_recv, rs_send, rs_recv, ag_send, ag_recv, g_send, g_recv,
):
    me_s = lax.axis_index("series")
    me_t = lax.axis_index("tm")
    rows, minutes = data_hbm.shape
    columns = omega_ref.shape[1]
    part = rows // CHUNKS
    steps, _ = halvings(columns, series)

    def chunk(c):
        return pl.ds(pl.multiple_of(c * part, part), part)

    def load(c):
        return (
            pltpu.make_async_copy(data_hbm.at[chunk(c)], data_v.at[chunk(c)], load_sem.at[0, c]),
            pltpu.make_async_copy(sparse_hbm.at[chunk(c)], sparse_v.at[chunk(c)], load_sem.at[1, c]),
        )

    for c in range(CHUNKS):
        for copy in load(c):
            copy.start()

    barrier = pltpu.get_barrier_semaphore()
    for d in range(1, tm):
        pl.semaphore_signal(
            barrier, inc=1, device_id=(me_s, lax.rem(me_t + d, tm)), device_id_type=MESH
        )
    for bit, _, _, _ in steps:
        low = lax.rem(me_s // bit, 2)
        pl.semaphore_signal(
            barrier, inc=1, device_id=(me_s + bit - 2 * bit * low, me_t), device_id_type=MESH
        )
    pl.semaphore_wait(barrier, tm - 1 + len(steps))

    def sketch_copy(c, d):
        return pltpu.make_async_remote_copy(
            src_ref=own.at[chunk(c)],
            dst_ref=arrived.at[d - 1, chunk(c)],
            send_sem=sk_send.at[d - 1, c],
            recv_sem=sk_recv.at[d - 1, c],
            device_id=(me_s, lax.rem(me_t + d, tm)),
            device_id_type=MESH,
        )

    def send_sketch(c, carry):
        for copy in load(c):
            copy.wait()
        residual = data_v[chunk(c), :] - sparse_v[chunk(c), :]
        data_v[chunk(c), :] = residual
        own[chunk(c), :] = jnp.dot(
            residual.astype(BF16), omega_ref[...], preferred_element_type=F32
        )
        for d in range(1, tm):
            sketch_copy(c, d).start()
        return carry

    lax.fori_loop(0, CHUNKS, send_sketch, 0)
    total[...] = jnp.zeros_like(total)

    def project(c, carry):
        for d in range(1, tm):
            sketch_copy(c, d).wait_recv()
        sketch = own[chunk(c), :]
        for d in range(1, tm):
            sketch = sketch + arrived[d - 1, chunk(c), :]
        sketch_ref[chunk(c), :] = sketch
        sketch_t = split(sketch.T)
        total[:, :minutes] += dot_split(sketch_t, split(data_v[chunk(c), :]))
        total[:, minutes:] += dot_split(sketch_t, split(sketch))
        return carry

    lax.fori_loop(0, CHUNKS, project, 0)

    start = me_s * 0
    offsets = []
    for turn, (bit, held, sent, place) in enumerate(steps):
        low = lax.rem(me_s // bit, 2)
        other = (me_s + bit - 2 * bit * low, me_t)
        if sent < held:
            keep, give = start + low * sent, start + (1 - low) * sent
        else:
            keep, give = start, start
        copy = pltpu.make_async_remote_copy(
            src_ref=total.at[pl.ds(pl.multiple_of(give, 8), sent)],
            dst_ref=halves.at[pl.ds(place, sent)],
            send_sem=rs_send.at[turn],
            recv_sem=rs_recv.at[turn],
            device_id=other,
            device_id_type=MESH,
        )
        copy.start()
        copy.wait()
        total[pl.ds(pl.multiple_of(keep, 8), sent), :] += halves[pl.ds(place, sent), :]
        offsets.append((keep, other))
        start = keep

    last = steps[-1][2]
    mine = pl.ds(pl.multiple_of(start, 8), last)
    sums_ref[mine, :] = total[mine, :]
    for turn in reversed(range(len(steps))):
        bit, held, sent, _ = steps[turn]
        if sent == held:
            continue
        keep, other = offsets[turn]
        piece = sums_ref.at[pl.ds(pl.multiple_of(keep, 8), sent)]
        copy = pltpu.make_async_remote_copy(
            src_ref=piece,
            dst_ref=piece,
            send_sem=ag_send.at[turn],
            recv_sem=ag_recv.at[turn],
            device_id=other,
            device_id_type=MESH,
        )
        copy.start()
        copy.wait()

    product = split(sums_ref[:, :minutes])
    gram_own[...] = dot_split(product, product, ((1,), (1,)))
    copies = []
    for d in range(1, tm):
        copy = pltpu.make_async_remote_copy(
            src_ref=gram_own,
            dst_ref=gram_in.at[d - 1],
            send_sem=g_send.at[d - 1],
            recv_sem=g_recv.at[d - 1],
            device_id=(me_s, lax.rem(me_t + d, tm)),
            device_id_type=MESH,
        )
        copy.start()
        copies.append(copy)
    for copy in copies:
        copy.wait()
    gram = gram_own[...]
    for d in range(1, tm):
        gram = gram + gram_in[d - 1]
    gram_ref[...] = gram

    def sent_sketch(c, carry):
        for d in range(1, tm):
            sketch_copy(c, d).wait_send()
        return carry

    lax.fori_loop(0, CHUNKS, sent_sketch, 0)


def total_of(x):
    return jnp.sum(jnp.sum(x, axis=1, keepdims=True), axis=0, keepdims=True)


def shrink_into(sums_ref, gram_ref, scale, coef_ref):
    minutes = coef_ref.shape[1]
    columns = gram_ref.shape[0]
    shape = (columns, columns)
    row = lax.broadcasted_iota(jnp.int32, shape, 0)
    col = lax.broadcasted_iota(jnp.int32, shape, 1)
    identity = jnp.where(row == col, 1.0, 0.0).astype(F32)

    def coupled(root, inverse):
        inverse_s, root_s = split(inverse), split(root)
        middle = 1.5 * identity - 0.5 * dot_split(inverse_s, root_s)
        middle_s = split(middle)
        return dot_split(root_s, middle_s), dot_split(middle_s, inverse_s), middle

    first = sums_ref[:, minutes:]
    size = 0.5 * jnp.sqrt(total_of(first * first))

    def basis_on(state):
        counter, error, _, _ = state
        return jnp.logical_and(counter < BASIS_STEPS, error > 2.5e-5)

    def basis_turn(state):
        counter, _, root, inverse = state
        root, inverse, middle = coupled(root, inverse)
        away = middle - identity
        return counter + 1, jnp.sum(away * away), root, inverse

    _, _, _, whiten = lax.while_loop(
        basis_on, basis_turn, (jnp.int32(0), jnp.float32(1.0), first / size, identity)
    )
    whiten = whiten * lax.rsqrt(size)
    whiten_s = split(whiten)
    gram = dot_split(split(dot_split(whiten_s, split(gram_ref[...]))), whiten_s)
    gram = 0.5 * (gram + gram.T)

    magnitude = jnp.sqrt(total_of(gram * gram))
    trace = total_of(gram * identity)
    threshold = scale * jnp.sqrt(trace / columns)
    root, inverse = lax.fori_loop(
        0, ROOT_STEPS, lambda i, s: coupled(*s)[:2], (gram / magnitude, identity)
    )
    root_scale = jnp.sqrt(magnitude)
    shifted = root_scale * root - threshold * identity
    signed = shifted / jnp.sqrt(total_of(shifted * shifted) + 1e-06)

    def sign_turn(i, x):
        x_s = split(x)
        return 1.5 * x - 0.5 * dot_split(x_s, split(dot_split(x_s, x_s)))

    signed = lax.fori_loop(0, SIGN_STEPS, sign_turn, signed)
    factor = 0.5 * mm(identity + signed, identity - threshold / root_scale * inverse)
    inner = mm(dot_split(whiten_s, split(factor)), whiten)
    coef_ref[...] = mm(inner, sums_ref[:, :minutes])


def finish_kernel(sums_ref, gram_ref, scale_ref, cut_ref, sketch_ref, data_ref, low_ref, out_ref, high, rest, coef):
    @pl.when(pl.program_id(0) == 0)
    def _():
        shrink_into(sums_ref, gram_ref, scale_ref[0], coef)
        high[...], rest[...] = split(coef[...])

    low_rank = dot_split(split(sketch_ref[...]), (high[...], rest[...]))
    low_ref[...] = low_rank
    gap = data_ref[...] - low_rank
    size = jnp.maximum(jnp.abs(gap) - cut_ref[0], 0.0)
    out_ref[...] = jnp.where(gap < 0, -size, size)


def on_device(series, tm, data, sparse, omega, svt_scale, sparse_threshold):
    rows, minutes = data.shape
    columns = omega.shape[1]
    wide = minutes + columns
    steps, arrivals = halvings(columns, series)
    turns = len(steps)
    vmem = pl.BlockSpec(memory_space=pltpu.VMEM)
    hbm = pl.BlockSpec(memory_space=pl.ANY)
    dma = pltpu.SemaphoreType.DMA
    sketch, sums, gram = pl.pallas_call(
        functools.partial(gather_kernel, series, tm),
        out_shape=(
            jax.ShapeDtypeStruct((rows, columns), F32),
            jax.ShapeDtypeStruct((columns, wide), F32),
            jax.ShapeDtypeStruct((columns, columns), F32),
        ),
        in_specs=[hbm, hbm, vmem],
        out_specs=(vmem, vmem, vmem),
        scratch_shapes=[
            pltpu.VMEM((rows, minutes), F32),
            pltpu.VMEM((rows, minutes), F32),
            pltpu.VMEM((rows, columns), F32),
            pltpu.VMEM((tm - 1, rows, columns), F32),
            pltpu.VMEM((columns, wide), F32),
            pltpu.VMEM((arrivals, wide), F32),
            pltpu.VMEM((columns, columns), F32),
            pltpu.VMEM((tm - 1, columns, columns), F32),
            dma((2, CHUNKS)),
            dma((tm - 1, CHUNKS)),
            dma((tm - 1, CHUNKS)),
            dma((turns,)),
            dma((turns,)),
            dma((turns,)),
            dma((turns,)),
            dma((tm - 1,)),
            dma((tm - 1,)),
        ],
        compiler_params=pltpu.CompilerParams(
            collective_id=0, has_side_effects=True, vmem_limit_bytes=44 * 2**20
        ),
        name="gather",
    )(data, sparse, omega)
    block = rows // 8
    smem = pl.BlockSpec(memory_space=pltpu.SMEM)
    return pl.pallas_call(
        finish_kernel,
        grid=(rows // block,),
        out_shape=(
            jax.ShapeDtypeStruct((rows, minutes), F32),
            jax.ShapeDtypeStruct((rows, minutes), F32),
        ),
        in_specs=[
            pl.BlockSpec((columns, wide), lambda i: (0, 0)),
            pl.BlockSpec((columns, columns), lambda i: (0, 0)),
            smem,
            smem,
            pl.BlockSpec((block, columns), lambda i: (i, 0)),
            pl.BlockSpec((block, minutes), lambda i: (i, 0)),
        ],
        out_specs=(
            pl.BlockSpec((block, minutes), lambda i: (i, 0)),
            pl.BlockSpec((block, minutes), lambda i: (i, 0)),
        ),
        scratch_shapes=[
            pltpu.VMEM((columns, minutes), BF16),
            pltpu.VMEM((columns, minutes), BF16),
            pltpu.VMEM((columns, minutes), F32),
        ],
        compiler_params=pltpu.CompilerParams(vmem_limit_bytes=44 * 2**20),
        name="finish",
    )(sums, gram, svt_scale, sparse_threshold, sketch, data)


def solution(mesh):
    placed = (P("series", "tm"), P("series", "tm"), P("tm", None), P(), P())
    return jax.shard_map(
        functools.partial(on_device, mesh.shape["series"], mesh.shape["tm"]),
        mesh=mesh,
        in_specs=placed,
        out_specs=(P("series", "tm"), P("series", "tm")),
        check_vma=False,
    )
```

time: 398 us -> 112 us (0.28)
  waiting for transfers between devices: 247 us -> 0 us
  Pallas kernels: 0 us -> 107 us
  other arithmetic: 62.5 us -> 0 us
  matrix products: 59.8 us -> 0 us
  between operations: 18.7 us -> 1.94 us
  local copies, waits for them, and re-layouts: 8.45 us -> 3.22 us
    psum x4 -> x0, waiting for transfers between devices: 247 us -> none  [the longest x1 93.8 us: on_device(): lax.psum(jnp.dot(basis_t, residual, precision=highest), 'series')]
    pallas_call x0 -> x2, Pallas kernels: none -> 107 us  [the longest x1 76.6 us: on_device(): pl.pallas_call(functools.partial(gather_kernel, series, tm), out_shape=(j...]
    dot_general x67 -> x0, matrix products: 57.1 us -> none  [the longest x1 8.75 us: on_device(): jnp.dot(basis_t.T, jnp.dot(factor, projection, precision=highest), precis...]
    another operation x9 -> x0, other arithmetic: 53.7 us -> none  [the longest x6 34 us: on_device(): basis_t = lower_solve(jnp.linalg.cholesky(gram_first), sketch_t)]
    sub x1 -> x0, other arithmetic: 4.43 us -> none  [on_device(): residual = data - sparse]
    another operation x9 -> x0, local copies, waits for them, and re-layouts: 4.15 us -> none
  transfers between devices with their start and end apart: 4 -> 0, of which waited for: 4 -> 0; matrix products, arithmetic and copies ran while one was open for 0% -> 0% of each run, Pallas kernels for 0% -> 0%
where the time goes in v1:
time: 112 us
  Pallas kernels  107 us (96%)
  local copies, waits for them, and re-layouts  3.22 us (3%)
  between operations  1.94 us (2%)
    pallas_call x1, Pallas kernels, on_device(): pl.pallas_call(functools.partial(gather_kernel, series, tm), out_shape=(j...  76.6 us
    pallas_call x1, Pallas kernels, on_device(): pl.pallas_call(finish_kernel, grid=(rows // block,), out_shape=(jax.Shape...  30.4 us
    unnamed x4, local copies, waits for them, and re-layouts  3.22 us

profile of v1, /device:TPU:0, one launch (start us, length us, event | category | flops | bytes accessed | tf_op | source)
XLA Modules:
  0.0 112.2 jit_solution(17644759473294575572)
XLA Ops:
  1.9 0.0 copy-start
  1.9 2.2 %copy-done = f32[1024,1024]{1,0:T(8,128)S(1)} copy-done((f32[1024,1024]{1,0:T(8,128)S(1)}, f32[1024,1024]{1,0:T(8,128)}, u32[]{:S(2)}) %copy-start) | copy-done | bytes 4194328
  4.1 0.0 copy-start.1
  4.1 1.0 copy-done.1
  5.2 76.6 %gather.1 = (f32[1024,256]{1,0:T(8,128)S(1)}, f32[256,1280]{1,0:T(8,128)S(1)}, f32[256,256]{1,0:T(8,128)S(1)}) custom-call(f32[1024,1024]{1,0:T(8,128)S(1)} %copy-done, f32[1024,1024]{1,0:T(8,128)} %sparse_hbm.1, bf16[1024,256]{1,0:T(8,128)(2,1)S(1)} %copy-done.1), custom_call_target="tpu_custom_call" | custom-call | tf_op jit(solution)/shard_map/gather/pallas_call | solution.py:276
  81.8 30.4 %finish.1 = (f32[1024,1024]{1,0:T(8,128)}, f32[1024,1024]{1,0:T(8,128)}) custom-call(f32[256,1280]{1,0:T(8,128)S(1)} %get-tuple-element.5.sums_ref, f32[256,256]{1,0:T(8,128)S(1)} %get-tuple-element.6.gram_ref, f32[1]{0:T(128)S(6)} %copy.7.scale_ref, f32[1]{0:T(128)S(6)} %copy.8.cut_ref, f32[1024,256]{1,0:T(8,128)S(1)} %get-tuple-element.7.sketch_ref, ...), custom_call_target="tpu_custom_call" | custom-call | tf_op jit(solution)/shard_map/finish/pallas_call | solution.py:311
Async XLA Ops:
  1.9 2.2 %copy-start = (f32[1024,1024]{1,0:T(8,128)S(1)}, f32[1024,1024]{1,0:T(8,128)}, u32[]{:S(2)}) copy-start(f32[1024,1024]{1,0:T(8,128)} %data_ref.1) | copy-start | bytes 12582916
  4.1 1.0 copy-start.1

commit v2 on v0

v2 whole, which is shorter than its diff:
```python
import functools

import jax
import jax.numpy as jnp
from jax import lax
from jax.experimental import pallas as pl
from jax.experimental.pallas import tpu as pltpu
from jax.sharding import PartitionSpec as P

ROOT_STEPS = 12
SIGN_STEPS = 12
QUINTIC_STEPS = 6
CUBIC_STEPS = 4
CHUNKS = 4
LANES = 128
F32 = jnp.float32
BF16 = jnp.bfloat16
MESH = pl.DeviceIdType.MESH


def split(x):
    high = x.astype(BF16)
    return high, (x - high.astype(F32)).astype(BF16)


def dot_split(a, b, dims=((1,), (0,))):
    mul = functools.partial(
        lax.dot_general, dimension_numbers=(dims, ((), ())), preferred_element_type=F32
    )
    (ah, al), (bh, bl) = a, b
    return mul(ah, bh) + (mul(ah, bl) + mul(al, bh))


def mm(a, b):
    return dot_split(split(a), split(b))


def total_of(x):
    return jnp.sum(jnp.sum(x, axis=1, keepdims=True), axis=0, keepdims=True)


def eye(columns):
    shape = (columns, columns)
    row = lax.broadcasted_iota(jnp.int32, shape, 0)
    col = lax.broadcasted_iota(jnp.int32, shape, 1)
    return jnp.where(row == col, 1.0, 0.0).astype(F32)


def apply(root_s, inverse_s, middle):
    middle_s = split(middle)
    return dot_split(root_s, middle_s), dot_split(middle_s, inverse_s)


def cubic(identity, state):
    root_s, inverse_s = split(state[0]), split(state[1])
    return apply(root_s, inverse_s, 1.5 * identity - 0.5 * dot_split(inverse_s, root_s))


def quintic(identity, state):
    root_s, inverse_s = split(state[0]), split(state[1])
    both = dot_split(inverse_s, root_s)
    both_s = split(both)
    middle = 3.4445 * identity - 4.775 * both + 2.0315 * dot_split(both_s, both_s)
    return apply(root_s, inverse_s, middle)


def whitener(first):
    identity = eye(first.shape[0])
    size = jnp.sqrt(total_of(first * first))
    state = (first / size, identity)
    state = lax.fori_loop(0, QUINTIC_STEPS, lambda i, s: quintic(identity, s), state)
    state = lax.fori_loop(0, CUBIC_STEPS, lambda i, s: cubic(identity, s), state)
    return state[1] * lax.rsqrt(size)


def stack(ref, value):
    columns = value.shape[0]
    for k in range(columns // LANES):
        ref[k * columns : (k + 1) * columns, :] = value[:, k * LANES : (k + 1) * LANES]


def unstack(ref, columns):
    return jnp.concatenate(
        [ref[k * columns : (k + 1) * columns, :] for k in range(columns // LANES)], axis=1
    )


def gather_kernel(
    series, tm, data_hbm, sparse_hbm, omega_ref, scale_ref, sketch_ref, high_ref, rest_ref,
    data_v, sparse_v, turned_h, turned_l, own, arrived,
    proj, proj_pair, proj_in, proj_all,
    first, first_pair, first_in, first_all,
    gram, gram_pair, gram_in, gram_tm, gram_all,
    load_sem, sk_sem, proj_sem, first_sem, gram_sem, gram_tm_sem,
):
    me_s = lax.axis_index("series")
    me_t = lax.axis_index("tm")
    core = lax.rem(me_s, 2)
    chip = me_s // 2
    chips = series // 2
    pair = (me_s + 1 - 2 * core, me_t)
    rows, minutes = data_hbm.shape
    columns = omega_ref.shape[1]
    part = rows // CHUNKS

    def chunk(c):
        return pl.ds(pl.multiple_of(c * part, part), part)

    def load(c):
        return (
            pltpu.make_async_copy(data_hbm.at[chunk(c)], data_v.at[chunk(c)], load_sem.at[0, c]),
            pltpu.make_async_copy(sparse_hbm.at[chunk(c)], sparse_v.at[chunk(c)], load_sem.at[1, c]),
        )

    for c in range(CHUNKS):
        for copy in load(c):
            copy.start()

    def peer(d):
        return lax.rem(chip + d, chips)

    barrier = pltpu.get_barrier_semaphore()
    for d in range(1, tm):
        pl.semaphore_signal(
            barrier, inc=1, device_id=(me_s, lax.rem(me_t + d, tm)), device_id_type=MESH
        )
    pl.semaphore_signal(barrier, inc=1, device_id=pair, device_id_type=MESH)
    for d in range(1, chips):
        pl.semaphore_signal(
            barrier, inc=1, device_id=(2 * peer(d) + core, me_t), device_id_type=MESH
        )
    pl.semaphore_wait(barrier, tm - 1 + 1 + chips - 1)

    def remote(src, dst, sem, index, device):
        return pltpu.make_async_remote_copy(
            src_ref=src, dst_ref=dst, send_sem=sem.at[0, index], recv_sem=sem.at[1, index],
            device_id=device, device_id_type=MESH,
        )

    def span(start, size):
        return pl.ds(pl.multiple_of(start, 8), size)

    def pair_out(buf, inbox, sem):
        half = buf.shape[0] // 2
        return [remote(buf.at[span((1 - core) * half, half)], inbox, sem, 0, pair)]

    def pair_add(buf, inbox):
        half = buf.shape[0] // 2
        buf[span(core * half, half), :] += inbox[...]

    def chips_out(buf, inbox, sem):
        half, piece = buf.shape[0] // 2, buf.shape[0] // series
        return [
            remote(
                buf.at[span(core * half + peer(d) * piece, piece)],
                inbox.at[pl.ds((d - 1) * piece, piece)],
                sem, d, (2 * peer(d) + core, me_t),
            )
            for d in range(1, chips)
        ]

    def mine(buf):
        half, piece = buf.shape[0] // 2, buf.shape[0] // series
        return span(core * half + chip * piece, piece)

    def chips_add(buf, inbox):
        piece = buf.shape[0] // series
        value = buf[mine(buf), :]
        for d in range(1, chips):
            value = value + inbox[(d - 1) * piece : d * piece, :]
        return value

    def chips_back(out, sem):
        here = out.at[mine(out)]
        return [
            remote(here, here, sem, chips + d, (2 * peer(d) + core, me_t)) for d in range(1, chips)
        ]

    def pair_back(out, sem):
        half = out.shape[0] // 2
        here = out.at[span(core * half, half)]
        return [remote(here, here, sem, chips, pair)]

    def start(copies):
        for copy in copies:
            copy.start()
        return copies

    def wait(copies):
        for copy in copies:
            copy.wait()

    def sketch_copy(c, d):
        return pltpu.make_async_remote_copy(
            src_ref=own.at[chunk(c)],
            dst_ref=arrived.at[d - 1, chunk(c)],
            send_sem=sk_sem.at[0, d - 1, c],
            recv_sem=sk_sem.at[1, d - 1, c],
            device_id=(me_s, lax.rem(me_t + d, tm)),
            device_id_type=MESH,
        )

    def send_sketch(c, carry):
        for copy in load(c):
            copy.wait()
        residual = data_v[chunk(c), :] - sparse_v[chunk(c), :]
        data_v[chunk(c), :] = residual
        own[chunk(c), :] = jnp.dot(
            residual.astype(BF16), omega_ref[...], preferred_element_type=F32
        )
        for d in range(1, tm):
            sketch_copy(c, d).start()
        return carry

    lax.fori_loop(0, CHUNKS, send_sketch, 0)

    def turn(c, carry):
        turned_h[:, chunk(c)], turned_l[:, chunk(c)] = split(data_v[chunk(c), :].T)
        return carry

    lax.fori_loop(0, CHUNKS, turn, 0)
    proj[...] = jnp.zeros_like(proj)

    def project(c, whole):
        for d in range(1, tm):
            sketch_copy(c, d).wait_recv()
        sketch = own[chunk(c), :]
        for d in range(1, tm):
            sketch = sketch + arrived[d - 1, chunk(c), :]
        sketch_ref[chunk(c), :] = sketch
        sketch_s = split(sketch)
        proj[...] += dot_split((turned_h[:, chunk(c)], turned_l[:, chunk(c)]), sketch_s)
        return whole + dot_split(split(sketch.T), sketch_s)

    stack(first, lax.fori_loop(0, CHUNKS, project, jnp.zeros((columns, columns), F32)))

    first_out = start(pair_out(first, first_pair, first_sem))
    proj_out = start(pair_out(proj, proj_pair, proj_sem))
    wait(first_out)
    pair_add(first, first_pair)
    first_out = start(chips_out(first, first_in, first_sem))
    wait(proj_out)
    pair_add(proj, proj_pair)
    proj_out = start(chips_out(proj, proj_in, proj_sem))
    wait(first_out)
    first_all[mine(first_all), :] = chips_add(first, first_in)
    wait(start(chips_back(first_all, first_sem)))
    wait(start(pair_back(first_all, first_sem)))

    whiten_s = split(whitener(unstack(first_all, columns)))

    wait(proj_out)
    proj_all[mine(proj_all), :] = chips_add(proj, proj_in)
    proj_out = chips_back(proj_all, proj_sem)
    piece_t = split(proj_all[mine(proj_all), :].T)
    stack(gram, dot_split(piece_t, piece_t, ((1,), (1,))))
    wait(start(pair_out(gram, gram_pair, gram_sem)))
    pair_add(gram, gram_pair)
    wait(start(chips_out(gram, gram_in, gram_sem)))
    value = chips_add(gram, gram_in)
    gram[mine(gram), :] = value
    copies = start(
        [
            remote(
                gram.at[mine(gram)], gram_tm.at[d - 1], gram_tm_sem, d - 1,
                (me_s, lax.rem(me_t + d, tm)),
            )
            for d in range(1, tm)
        ]
    )
    wait(copies)
    for d in range(1, tm):
        value = value + gram_tm[d - 1]
    gram_all[mine(gram_all), :] = value
    wait(start(chips_back(gram_all, gram_sem)))
    wait(start(pair_back(gram_all, gram_sem)))
    start(proj_out)

    identity = eye(columns)
    projected = dot_split(
        split(dot_split(whiten_s, split(unstack(gram_all, columns)))), whiten_s
    )
    projected = 0.5 * (projected + projected.T)
    magnitude = jnp.sqrt(total_of(projected * projected))
    threshold = scale_ref[0] * jnp.sqrt(total_of(projected * identity) / columns)
    root, inverse = lax.fori_loop(
        0, ROOT_STEPS, lambda i, s: cubic(identity, s), (projected / magnitude, identity)
    )
    root_scale = jnp.sqrt(magnitude)
    shifted = root_scale * root - threshold * identity
    signed = shifted / jnp.sqrt(total_of(shifted * shifted) + 1e-06)

    wait(proj_out)
    proj_out = start(pair_back(proj_all, proj_sem))

    def sign_turn(i, x):
        x_s = split(x)
        return 1.5 * x - 0.5 * dot_split(x_s, split(dot_split(x_s, x_s)))

    signed = lax.fori_loop(0, SIGN_STEPS, sign_turn, signed)
    factor = 0.5 * mm(identity + signed, identity - threshold / root_scale * inverse)
    inner_s = split(dot_split(split(dot_split(whiten_s, split(factor))), whiten_s))

    wait(proj_out)
    high_ref[...], rest_ref[...] = split(
        dot_split(split(proj_all[...]), inner_s, ((1,), (1,)))
    )

    def sent_sketch(c, carry):
        for d in range(1, tm):
            sketch_copy(c, d).wait_send()
        return carry

    lax.fori_loop(0, CHUNKS, sent_sketch, 0)


def finish_kernel(cut_ref, sketch_ref, high_ref, rest_ref, data_ref, low_ref, out_ref):
    low_rank = dot_split(
        split(sketch_ref[...]), (high_ref[...], rest_ref[...]), ((1,), (1,))
    )
    low_ref[...] = low_rank
    gap = data_ref[...] - low_rank
    size = jnp.maximum(jnp.abs(gap) - cut_ref[0], 0.0)
    out_ref[...] = jnp.where(gap < 0, -size, size)


def on_device(series, tm, data, sparse, omega, svt_scale, sparse_threshold):
    rows, minutes = data.shape
    columns = omega.shape[1]
    chips = series // 2
    stacked = columns * columns // LANES
    vmem = pl.BlockSpec(memory_space=pltpu.VMEM)
    hbm = pl.BlockSpec(memory_space=pltpu.HBM)
    smem = pl.BlockSpec(memory_space=pltpu.SMEM)
    dma = pltpu.SemaphoreType.DMA

    def inboxes(length, width):
        piece = length // series
        return [
            pltpu.VMEM((length, width), F32),
            pltpu.VMEM((length // 2, width), F32),
            pltpu.VMEM(((chips - 1) * piece, width), F32),
        ]

    sketch, high, rest = pl.pallas_call(
        functools.partial(gather_kernel, series, tm),
        out_shape=(
            jax.ShapeDtypeStruct((rows, columns), F32),
            jax.ShapeDtypeStruct((minutes, columns), BF16),
            jax.ShapeDtypeStruct((minutes, columns), BF16),
        ),
        in_specs=[hbm, hbm, vmem, smem],
        out_specs=(vmem, vmem, vmem),
        scratch_shapes=[
            pltpu.VMEM((rows, minutes), F32),
            pltpu.VMEM((rows, minutes), F32),
            pltpu.VMEM((minutes, rows), BF16),
            pltpu.VMEM((minutes, rows), BF16),
            pltpu.VMEM((rows, columns), F32),
            pltpu.VMEM((tm - 1, rows, columns), F32),
            *inboxes(minutes, columns),
            pltpu.VMEM((minutes, columns), F32),
            *inboxes(stacked, LANES),
            pltpu.VMEM((stacked, LANES), F32),
            *inboxes(stacked, LANES),
            pltpu.VMEM((tm - 1, stacked // series, LANES), F32),
            pltpu.VMEM((stacked, LANES), F32),
            dma((2, CHUNKS)),
            dma((2, tm - 1, CHUNKS)),
            dma((2, 2 * chips)),
            dma((2, 2 * chips)),
            dma((2, 2 * chips)),
            dma((2, tm - 1)),
        ],
        compiler_params=pltpu.CompilerParams(
            collective_id=0, has_side_effects=True, vmem_limit_bytes=48 * 2**20
        ),
        name="gather",
    )(data, sparse, omega, svt_scale)
    block = rows // 8
    return pl.pallas_call(
        finish_kernel,
        grid=(rows // block,),
        out_shape=(
            jax.ShapeDtypeStruct((rows, minutes), F32),
            jax.ShapeDtypeStruct((rows, minutes), F32),
        ),
        in_specs=[
            smem,
            pl.BlockSpec((block, columns), lambda i: (i, 0)),
            pl.BlockSpec((minutes, columns), lambda i: (0, 0)),
            pl.BlockSpec((minutes, columns), lambda i: (0, 0)),
            pl.BlockSpec((block, minutes), lambda i: (i, 0)),
        ],
        out_specs=(
            pl.BlockSpec((block, minutes), lambda i: (i, 0)),
            pl.BlockSpec((block, minutes), lambda i: (i, 0)),
        ),
        compiler_params=pltpu.CompilerParams(vmem_limit_bytes=48 * 2**20),
        name="finish",
    )(sparse_threshold, sketch, high, rest, data)


def solution(mesh):
    placed = (P("series", "tm"), P("series", "tm"), P("tm", None), P(), P())
    return jax.shard_map(
        functools.partial(on_device, mesh.shape["series"], mesh.shape["tm"]),
        mesh=mesh,
        in_specs=placed,
        out_specs=(P("series", "tm"), P("series", "tm")),
        check_vma=False,
    )
```

time: 398 us -> 111 us (0.28)
  waiting for transfers between devices: 247 us -> 0 us
  Pallas kernels: 0 us -> 107 us
  other arithmetic: 62.5 us -> 0 us
  matrix products: 59.8 us -> 0 us
  between operations: 18.7 us -> 1.94 us
  local copies, waits for them, and re-layouts: 8.45 us -> 1.03 us
    psum x4 -> x0, waiting for transfers between devices: 247 us -> none  [the longest x1 93.8 us: on_device(): lax.psum(jnp.dot(basis_t, residual, precision=highest), 'series')]
    pallas_call x0 -> x2, Pallas kernels: none -> 107 us  [the longest x1 97.2 us: on_device(): pl.pallas_call(functools.partial(gather_kernel, series, tm), out_shape=(j...]
    dot_general x67 -> x0, matrix products: 57.1 us -> none  [the longest x1 8.75 us: on_device(): jnp.dot(basis_t.T, jnp.dot(factor, projection, precision=highest), precis...]
    another operation x9 -> x0, other arithmetic: 53.7 us -> none  [the longest x6 34 us: on_device(): basis_t = lower_solve(jnp.linalg.cholesky(gram_first), sketch_t)]
    sub x1 -> x0, other arithmetic: 4.43 us -> none  [on_device(): residual = data - sparse]
    another operation x9 -> x0, local copies, waits for them, and re-layouts: 4.15 us -> none
  transfers between devices with their start and end apart: 4 -> 0, of which waited for: 4 -> 0; matrix products, arithmetic and copies ran while one was open for 0% -> 0% of each run, Pallas kernels for 0% -> 0%
where the time goes in v2:
time: 111 us; the launch traced here: 110 us
  Pallas kernels  107 us (96%)
  between operations  1.94 us (2%)
    pallas_call x1, Pallas kernels, on_device(): pl.pallas_call(functools.partial(gather_kernel, series, tm), out_shape=(j...  97.2 us
    pallas_call x1, Pallas kernels, on_device(): pl.pallas_call(finish_kernel, grid=(rows // block,), out_shape=(jax.Shape...  9.64 us

profile of v2, /device:TPU:0, one launch (start us, length us, event | category | flops | bytes accessed | tf_op | source)
XLA Modules:
  0.0 109.8 jit_solution(9366268103019807048)
XLA Ops:
  1.9 0.0 copy-start
  1.9 1.0 copy-done
  3.0 97.2 %gather.1 = (f32[1024,256]{1,0:T(8,128)S(1)}, bf16[1024,256]{1,0:T(8,128)(2,1)S(1)}, bf16[1024,256]{1,0:T(8,128)(2,1)S(1)}) custom-call(f32[1024,1024]{1,0:T(8,128)} %data_ref.1, f32[1024,1024]{1,0:T(8,128)} %sparse_hbm.1, bf16[1024,256]{1,0:T(8,128)(2,1)S(1)} %copy-done, f32[1]{0:T(128)S(6)} %copy.7.scale_ref), custom_call_target="tpu_custom_call" | custom-call | tf_op jit(solution)/shard_map/gather/pallas_call | solution.py:345
  100.2 9.6 %finish.1 = (f32[1024,1024]{1,0:T(8,128)}, f32[1024,1024]{1,0:T(8,128)}) custom-call(f32[1]{0:T(128)S(6)} %copy.8.cut_ref, f32[1024,256]{1,0:T(8,128)S(1)} %get-tuple-element.5.sketch_ref, bf16[1024,256]{1,0:T(8,128)(2,1)S(1)} %get-tuple-element.6.high_ref, bf16[1024,256]{1,0:T(8,128)(2,1)S(1)} %get-tuple-element.7.rest_ref, f32[1024,1024]{1,0:T(8,128)} %data_ref.1), custom_call_target="tpu_custom_call" | custom-call | tf_op jit(solution)/shard_map/finish/pallas_call | solution.py:381
Async XLA Ops:
  1.9 1.0 copy-start

commit v3 on v2

--- a/solution.py
+++ b/solution.py
@@ -64,13 +64,10 @@
     return apply(root_s, inverse_s, middle)
 
 
-def whitener(first):
-    identity = eye(first.shape[0])
+def whiten_turns(first, identity):
     size = jnp.sqrt(total_of(first * first))
-    state = (first / size, identity)
-    state = lax.fori_loop(0, QUINTIC_STEPS, lambda i, s: quintic(identity, s), state)
-    state = lax.fori_loop(0, CUBIC_STEPS, lambda i, s: cubic(identity, s), state)
-    return state[1] * lax.rsqrt(size)
+    turns = [quintic] * QUINTIC_STEPS + [cubic] * CUBIC_STEPS
+    return size, (first / size, identity), turns
 
 
 def stack(ref, value):
@@ -86,12 +83,12 @@
 
 
 def gather_kernel(
-    series, tm, data_hbm, sparse_hbm, omega_ref, scale_ref, sketch_ref, high_ref, rest_ref,
-    data_v, sparse_v, turned_h, turned_l, own, arrived,
+    series, tm, data_hbm, sparse_hbm, omega_hbm, scale_ref, sketch_ref, high_ref, rest_ref,
+    omega_ref, data_v, sparse_v, turned_h, turned_l, own, arrived,
     proj, proj_pair, proj_in, proj_all,
-    first, first_pair, first_in, first_all,
+    first_sum, first, first_pair, first_in, first_all,
     gram, gram_pair, gram_in, gram_tm, gram_all,
-    load_sem, sk_sem, proj_sem, first_sem, gram_sem, gram_tm_sem,
+    omega_sem, load_sem, sk_sem, proj_sem, back_sem, first_sem, gram_sem, gram_tm_sem,
 ):
     me_s = lax.axis_index("series")
     me_t = lax.axis_index("tm")
@@ -112,6 +109,8 @@
             pltpu.make_async_copy(sparse_hbm.at[chunk(c)], sparse_v.at[chunk(c)], load_sem.at[1, c]),
         )
 
+    omega_load = pltpu.make_async_copy(omega_hbm, omega_ref, omega_sem)
+    omega_load.start()
     for c in range(CHUNKS):
         for copy in load(c):
             copy.start()
@@ -190,29 +189,40 @@
         for copy in copies:
             copy.wait()
 
-    def sketch_copy(c, d):
+    def sketch_copy(k, c, d):
         return pltpu.make_async_remote_copy(
-            src_ref=own.at[chunk(c)],
-            dst_ref=arrived.at[d - 1, chunk(c)],
-            send_sem=sk_sem.at[0, d - 1, c],
-            recv_sem=sk_sem.at[1, d - 1, c],
+            src_ref=own.at[k, chunk(c)],
+            dst_ref=arrived.at[d - 1, k, chunk(c)],
+            send_sem=sk_sem.at[0, d - 1, k, c],
+            recv_sem=sk_sem.at[1, d - 1, k, c],
             device_id=(me_s, lax.rem(me_t + d, tm)),
             device_id_type=MESH,
         )
+
+    blocks = columns // LANES
+    omega_load.wait()
 
     def send_sketch(c, carry):
         for copy in load(c):
             copy.wait()
         residual = data_v[chunk(c), :] - sparse_v[chunk(c), :]
         data_v[chunk(c), :] = residual
-        own[chunk(c), :] = jnp.dot(
-            residual.astype(BF16), omega_ref[...], preferred_element_type=F32
-        )
+        sketch = jnp.dot(residual.astype(BF16), omega_ref[...], preferred_element_type=F32)
+        for k in range(blocks):
+            own[k, chunk(c), :] = sketch[:, k * LANES : (k + 1) * LANES]
         for d in range(1, tm):
-            sketch_copy(c, d).start()
+            sketch_copy(0, c, d).start()
         return carry
 
     lax.fori_loop(0, CHUNKS, send_sketch, 0)
+
+    def send_rest(c, carry):
+        for k in range(1, blocks):
+            for d in range(1, tm):
+                sketch_copy(k, c, d).start()
+        return carry
+
+    lax.fori_loop(0, CHUNKS, send_rest, 0)
 
     def turn(c, carry):
         turned_h[:, chunk(c)], turned_l[:, chunk(c)] = split(data_v[chunk(c), :].T)
@@ -221,42 +231,71 @@
     lax.fori_loop(0, CHUNKS, turn, 0)
     proj[...] = jnp.zeros_like(proj)
 
-    def project(c, whole):
-        for d in range(1, tm):
-            sketch_copy(c, d).wait_recv()
-        sketch = own[chunk(c), :]
-        for d in range(1, tm):
-            sketch = sketch + arrived[d - 1, chunk(c), :]
-        sketch_ref[chunk(c), :] = sketch
-        sketch_s = split(sketch)
-        proj[...] += dot_split((turned_h[:, chunk(c)], turned_l[:, chunk(c)]), sketch_s)
-        return whole + dot_split(split(sketch.T), sketch_s)
-
-    stack(first, lax.fori_loop(0, CHUNKS, project, jnp.zeros((columns, columns), F32)))
-
+    def project(k):
+        lanes = pl.ds(k * LANES, LANES)
+
+        def turn_of(c, carry):
+            for d in range(1, tm):
+                sketch_copy(k, c, d).wait_recv()
+            sketch = own[k, chunk(c), :]
+            for d in range(1, tm):
+                sketch = sketch + arrived[d - 1, k, chunk(c), :]
+            sketch_ref[chunk(c), lanes] = sketch
+            sketch_s = split(sketch)
+            proj[k] += dot_split((turned_h[:, chunk(c)], turned_l[:, chunk(c)]), sketch_s)
+            if k == blocks - 1:
+                every = sketch_ref[chunk(c), :]
+                first_sum[...] += dot_split(split(every.T), split(every))
+            return carry
+
+        lax.fori_loop(0, CHUNKS, turn_of, 0)
+
+    first_sum[...] = jnp.zeros_like(first_sum)
+    proj_out = []
+    for k in range(blocks - 1):
+        project(k)
+        wait(start(pair_out(proj.at[k], proj_pair.at[k], proj_sem.at[k])))
+        pair_add(proj.at[k], proj_pair.at[k])
+        proj_out += start(chips_out(proj.at[k], proj_in.at[k], proj_sem.at[k]))
+    project(blocks - 1)
+    stack(first, first_sum[...])
+
+    tail = blocks - 1
     first_out = start(pair_out(first, first_pair, first_sem))
-    proj_out = start(pair_out(proj, proj_pair, proj_sem))
+    tail_out = start(pair_out(proj.at[tail], proj_pair.at[tail], proj_sem.at[tail]))
     wait(first_out)
     pair_add(first, first_pair)
     first_out = start(chips_out(first, first_in, first_sem))
-    wait(proj_out)
-    pair_add(proj, proj_pair)
-    proj_out = start(chips_out(proj, proj_in, proj_sem))
+    wait(tail_out)
+    pair_add(proj.at[tail], proj_pair.at[tail])
+    proj_out += start(chips_out(proj.at[tail], proj_in.at[tail], proj_sem.at[tail]))
     wait(first_out)
     first_all[mine(first_all), :] = chips_add(first, first_in)
     wait(start(chips_back(first_all, first_sem)))
     wait(start(pair_back(first_all, first_sem)))
 
-    whiten_s = split(whitener(unstack(first_all, columns)))
-
     wait(proj_out)
-    proj_all[mine(proj_all), :] = chips_add(proj, proj_in)
-    proj_out = chips_back(proj_all, proj_sem)
+    for k in range(blocks):
+        proj_all[mine(proj_all), pl.ds(k * LANES, LANES)] = chips_add(proj.at[k], proj_in.at[k])
     piece_t = split(proj_all[mine(proj_all), :].T)
     stack(gram, dot_split(piece_t, piece_t, ((1,), (1,))))
-    wait(start(pair_out(gram, gram_pair, gram_sem)))
+
+    identity = eye(columns)
+    size, state, turns = whiten_turns(unstack(first_all, columns), identity)
+    share = -(-len(turns) // 5)
+
+    def whiten_some(state, hop):
+        for turn_now in turns[hop * share : (hop + 1) * share]:
+            state = turn_now(identity, state)
+        return state
+
+    copies = start(pair_out(gram, gram_pair, gram_sem))
+    state = whiten_some(state, 0)
+    wait(copies)
     pair_add(gram, gram_pair)
-    wait(start(chips_out(gram, gram_in, gram_sem)))
+    copies = start(chips_out(gram, gram_in, gram_sem))
+    state = whiten_some(state, 1)
+    wait(copies)
     value = chips_add(gram, gram_in)
     gram[mine(gram), :] = value
     copies = start(
@@ -268,15 +307,20 @@
             for d in range(1, tm)
         ]
     )
+    state = whiten_some(state, 2)
     wait(copies)
     for d in range(1, tm):
         value = value + gram_tm[d - 1]
     gram_all[mine(gram_all), :] = value
-    wait(start(chips_back(gram_all, gram_sem)))
-    wait(start(pair_back(gram_all, gram_sem)))
-    start(proj_out)
-
-    identity = eye(columns)
+    copies = start(chips_back(gram_all, gram_sem))
+    proj_out = start(chips_back(proj_all, back_sem))
+    state = whiten_some(state, 3)
+    wait(copies)
+    copies = start(pair_back(gram_all, gram_sem))
+    state = whiten_some(state, 4)
+    whiten_s = split(state[1] * lax.rsqrt(size))
+    wait(copies)
+
     projected = dot_split(
         split(dot_split(whiten_s, split(unstack(gram_all, columns)))), whiten_s
     )
@@ -291,7 +335,7 @@
     signed = shifted / jnp.sqrt(total_of(shifted * shifted) + 1e-06)
 
     wait(proj_out)
-    proj_out = start(pair_back(proj_all, proj_sem))
+    proj_out = start(pair_back(proj_all, back_sem))
 
     def sign_turn(i, x):
         x_s = split(x)
@@ -303,12 +347,13 @@
 
     wait(proj_out)
     high_ref[...], rest_ref[...] = split(
-        dot_split(split(proj_all[...]), inner_s, ((1,), (1,)))
+        dot_split(inner_s, split(proj_all[...]), ((1,), (1,)))
     )
 
     def sent_sketch(c, carry):
-        for d in range(1, tm):
-            sketch_copy(c, d).wait_send()
+        for k in range(blocks):
+            for d in range(1, tm):
+                sketch_copy(k, c, d).wait_send()
         return carry
 
     lax.fori_loop(0, CHUNKS, sent_sketch, 0)
@@ -316,7 +361,7 @@
 
 def finish_kernel(cut_ref, sketch_ref, high_ref, rest_ref, data_ref, low_ref, out_ref):
     low_rank = dot_split(
-        split(sketch_ref[...]), (high_ref[...], rest_ref[...]), ((1,), (1,))
+        split(sketch_ref[...]), (high_ref[...], rest_ref[...])
     )
     low_ref[...] = low_rank
     gap = data_ref[...] - low_rank
@@ -334,39 +379,44 @@
     smem = pl.BlockSpec(memory_space=pltpu.SMEM)
     dma = pltpu.SemaphoreType.DMA
 
-    def inboxes(length, width):
-        piece = length // series
+    blocks = columns // LANES
+
+    def inboxes(*shape):
+        length = shape[-1]
         return [
-            pltpu.VMEM((length, width), F32),
-            pltpu.VMEM((length // 2, width), F32),
-            pltpu.VMEM(((chips - 1) * piece, width), F32),
+            pltpu.VMEM((*shape[:-1], size, LANES), F32)
+            for size in (length, length // 2, (chips - 1) * (length // series))
         ]
 
     sketch, high, rest = pl.pallas_call(
         functools.partial(gather_kernel, series, tm),
         out_shape=(
             jax.ShapeDtypeStruct((rows, columns), F32),
-            jax.ShapeDtypeStruct((minutes, columns), BF16),
-            jax.ShapeDtypeStruct((minutes, columns), BF16),
+            jax.ShapeDtypeStruct((columns, minutes), BF16),
+            jax.ShapeDtypeStruct((columns, minutes), BF16),
         ),
-        in_specs=[hbm, hbm, vmem, smem],
+        in_specs=[hbm, hbm, hbm, smem],
         out_specs=(vmem, vmem, vmem),
         scratch_shapes=[
+            pltpu.VMEM((minutes, columns), BF16),
             pltpu.VMEM((rows, minutes), F32),
             pltpu.VMEM((rows, minutes), F32),
             pltpu.VMEM((minutes, rows), BF16),
             pltpu.VMEM((minutes, rows), BF16),
-            pltpu.VMEM((rows, columns), F32),
-            pltpu.VMEM((tm - 1, rows, columns), F32),
-            *inboxes(minutes, columns),
+            pltpu.VMEM((blocks, rows, LANES), F32),
+            pltpu.VMEM((tm - 1, blocks, rows, LANES), F32),
+            *inboxes(blocks, minutes),
             pltpu.VMEM((minutes, columns), F32),
-            *inboxes(stacked, LANES),
+            pltpu.VMEM((columns, columns), F32),
+            *inboxes(stacked),
             pltpu.VMEM((stacked, LANES), F32),
-            *inboxes(stacked, LANES),
+            *inboxes(stacked),
             pltpu.VMEM((tm - 1, stacked // series, LANES), F32),
             pltpu.VMEM((stacked, LANES), F32),
+            dma,
             dma((2, CHUNKS)),
-            dma((2, tm - 1, CHUNKS)),
+            dma((2, tm - 1, blocks, CHUNKS)),
+            dma((blocks, 2, 2 * chips)),
             dma((2, 2 * chips)),
             dma((2, 2 * chips)),
             dma((2, 2 * chips)),
@@ -388,8 +438,8 @@
         in_specs=[
             smem,
             pl.BlockSpec((block, columns), lambda i: (i, 0)),
-            pl.BlockSpec((minutes, columns), lambda i: (0, 0)),
-            pl.BlockSpec((minutes, columns), lambda i: (0, 0)),
+            pl.BlockSpec((columns, minutes), lambda i: (0, 0)),
+            pl.BlockSpec((columns, minutes), lambda i: (0, 0)),
             pl.BlockSpec((block, minutes), lambda i: (i, 0)),
         ],
         out_specs=(

time: 111 us -> 104 us (0.937); the launches traced: 110 us -> 104 us
  Pallas kernels: 107 us -> 101 us
    pallas_call x1, Pallas kernels: 97.2 us -> 92.4 us  [on_device(): pl.pallas_call(functools.partial(gather_kernel, series, tm), out_shape=(j...]
where the time goes in v3:
time: 104 us
  Pallas kernels  101 us (97%)
  between operations  1.94 us (2%)
    pallas_call x1, Pallas kernels, on_device(): pl.pallas_call(functools.partial(gather_kernel, series, tm), out_shape=(j...  92.4 us
    pallas_call x1, Pallas kernels, on_device(): pl.pallas_call(finish_kernel, grid=(rows // block,), out_shape=(jax.Shape...  8.57 us

profile of v3, /device:TPU:0, one launch (start us, length us, event | category | flops | bytes accessed | tf_op | source)
XLA Modules:
  0.0 104.0 jit_solution(8588018552282389736)
XLA Ops:
  1.9 0.0 copy-start
  1.9 1.0 copy-done
  3.0 92.4 %gather.1 = (f32[1024,256]{1,0:T(8,128)S(1)}, bf16[256,1024]{1,0:T(8,128)(2,1)S(1)}, bf16[256,1024]{1,0:T(8,128)(2,1)S(1)}) custom-call(f32[1024,1024]{1,0:T(8,128)} %data_ref.1, f32[1024,1024]{1,0:T(8,128)} %sparse_hbm.1, bf16[1024,256]{1,0:T(8,128)(2,1)S(1)} %copy-done, f32[1]{0:T(128)S(6)} %copy.7.scale_ref), custom_call_target="tpu_custom_call" | custom-call | tf_op jit(solution)/shard_map/gather/pallas_call | solution.py:391
  95.4 8.6 %finish.1 = (f32[1024,1024]{1,0:T(8,128)}, f32[1024,1024]{1,0:T(8,128)}) custom-call(f32[1]{0:T(128)S(6)} %copy.8.cut_ref, f32[1024,256]{1,0:T(8,128)S(1)} %get-tuple-element.5.sketch_ref, bf16[256,1024]{1,0:T(8,128)(2,1)S(1)} %get-tuple-element.6.high_ref, bf16[256,1024]{1,0:T(8,128)(2,1)S(1)} %get-tuple-element.7.rest_ref, f32[1024,1024]{1,0:T(8,128)} %data_ref.1), custom_call_target="tpu_custom_call" | custom-call | tf_op jit(solution)/shard_map/finish/pallas_call | solution.py:431
Async XLA Ops:
  1.9 1.0 %copy-start = (bf16[1024,256]{1,0:T(8,128)(2,1)S(1)}, bf16[1024,256]{1,0:T(8,128)(2,1)}, u32[]{:S(2)}) copy-start(bf16[1024,256]{1,0:T(8,128)(2,1)} %omega_hbm.1) | copy-start | bytes 1572868

commit v4 on v3

--- a/solution.py
+++ b/solution.py
@@ -261,18 +261,14 @@
     stack(first, first_sum[...])
 
     tail = blocks - 1
+    tail_out = start(pair_out(proj.at[tail], proj_pair.at[tail], proj_sem.at[tail]))
     first_out = start(pair_out(first, first_pair, first_sem))
-    tail_out = start(pair_out(proj.at[tail], proj_pair.at[tail], proj_sem.at[tail]))
-    wait(first_out)
-    pair_add(first, first_pair)
-    first_out = start(chips_out(first, first_in, first_sem))
     wait(tail_out)
     pair_add(proj.at[tail], proj_pair.at[tail])
     proj_out += start(chips_out(proj.at[tail], proj_in.at[tail], proj_sem.at[tail]))
     wait(first_out)
-    first_all[mine(first_all), :] = chips_add(first, first_in)
-    wait(start(chips_back(first_all, first_sem)))
-    wait(start(pair_back(first_all, first_sem)))
+    pair_add(first, first_pair)
+    first_out = start(chips_out(first, first_in, first_sem))
 
     wait(proj_out)
     for k in range(blocks):
@@ -280,21 +276,26 @@
     piece_t = split(proj_all[mine(proj_all), :].T)
     stack(gram, dot_split(piece_t, piece_t, ((1,), (1,))))
 
-    identity = eye(columns)
-    size, state, turns = whiten_turns(unstack(first_all, columns), identity)
-    share = -(-len(turns) // 5)
-
-    def whiten_some(state, hop):
-        for turn_now in turns[hop * share : (hop + 1) * share]:
-            state = turn_now(identity, state)
-        return state
-
     copies = start(pair_out(gram, gram_pair, gram_sem))
-    state = whiten_some(state, 0)
+    wait(first_out)
+    first_all[mine(first_all), :] = chips_add(first, first_in)
+    first_out = start(chips_back(first_all, first_sem))
     wait(copies)
     pair_add(gram, gram_pair)
     copies = start(chips_out(gram, gram_in, gram_sem))
-    state = whiten_some(state, 1)
+    wait(first_out)
+    wait(start(pair_back(first_all, first_sem)))
+
+    identity = eye(columns)
+    size, state, turns = whiten_turns(unstack(first_all, columns), identity)
+    share = -(-len(turns) // 4)
+
+    def whiten_some(state, hop):
+        for turn_now in turns[max(0, hop * share - 2) : (hop + 1) * share - 2]:
+            state = turn_now(identity, state)
+        return state
+
+    state = whiten_some(state, 0)
     wait(copies)
     value = chips_add(gram, gram_in)
     gram[mine(gram), :] = value
@@ -307,17 +308,17 @@
             for d in range(1, tm)
         ]
     )
-    state = whiten_some(state, 2)
+    state = whiten_some(state, 1)
     wait(copies)
     for d in range(1, tm):
         value = value + gram_tm[d - 1]
     gram_all[mine(gram_all), :] = value
     copies = start(chips_back(gram_all, gram_sem))
+    state = whiten_some(state, 2)
+    wait(copies)
+    copies = start(pair_back(gram_all, gram_sem))
     proj_out = start(chips_back(proj_all, back_sem))
     state = whiten_some(state, 3)
-    wait(copies)
-    copies = start(pair_back(gram_all, gram_sem))
-    state = whiten_some(state, 4)
     whiten_s = split(state[1] * lax.rsqrt(size))
     wait(copies)
 
@@ -427,7 +428,7 @@
         ),
         name="gather",
     )(data, sparse, omega, svt_scale)
-    block = rows // 8
+    block = rows // 4
     return pl.pallas_call(
         finish_kernel,
         grid=(rows // block,),

time: 104 us -> 96.8 us (0.931)
  Pallas kernels: 101 us -> 93.6 us
    pallas_call x1, Pallas kernels: 92.4 us -> 86.7 us  [on_device(): pl.pallas_call(functools.partial(gather_kernel, series, tm), out_shape=(j...]
    pallas_call x1, Pallas kernels: 8.57 us -> 6.92 us  [on_device(): pl.pallas_call(finish_kernel, grid=(rows // block,), out_shape=(jax.Shape...]
where the time goes in v4:
time: 96.8 us; the launch traced here: 96.6 us
  Pallas kernels  93.6 us (97%)
  between operations  1.94 us (2%)
  local copies, waits for them, and re-layouts  1.03 us (1%)
    pallas_call x1, Pallas kernels, on_device(): pl.pallas_call(functools.partial(gather_kernel, series, tm), out_shape=(j...  86.7 us
    pallas_call x1, Pallas kernels, on_device(): pl.pallas_call(finish_kernel, grid=(rows // block,), out_shape=(jax.Shape...  6.92 us

profile of v4, /device:TPU:0, one launch (start us, length us, event | category | flops | bytes accessed | tf_op | source)
XLA Modules:
  0.0 96.6 jit_solution(12354249204464073545)
XLA Ops:
  1.9 0.0 copy-start
  1.9 1.0 %copy-done = bf16[1024,256]{1,0:T(8,128)(2,1)S(1)} copy-done((bf16[1024,256]{1,0:T(8,128)(2,1)S(1)}, bf16[1024,256]{1,0:T(8,128)(2,1)}, u32[]{:S(2)}) %copy-start) | copy-done | bytes 524312
  3.0 86.7 %gather.1 = (f32[1024,256]{1,0:T(8,128)S(1)}, bf16[256,1024]{1,0:T(8,128)(2,1)S(1)}, bf16[256,1024]{1,0:T(8,128)(2,1)S(1)}) custom-call(f32[1024,1024]{1,0:T(8,128)} %data_ref.1, f32[1024,1024]{1,0:T(8,128)} %sparse_hbm.1, bf16[1024,256]{1,0:T(8,128)(2,1)S(1)} %copy-done, f32[1]{0:T(128)S(6)} %copy.7.scale_ref), custom_call_target="tpu_custom_call" | custom-call | tf_op jit(solution)/shard_map/gather/pallas_call | solution.py:392
  89.6 6.9 %finish.1 = (f32[1024,1024]{1,0:T(8,128)}, f32[1024,1024]{1,0:T(8,128)}) custom-call(f32[1]{0:T(128)S(6)} %copy.8.cut_ref, f32[1024,256]{1,0:T(8,128)S(1)} %get-tuple-element.5.sketch_ref, bf16[256,1024]{1,0:T(8,128)(2,1)S(1)} %get-tuple-element.6.high_ref, bf16[256,1024]{1,0:T(8,128)(2,1)S(1)} %get-tuple-element.7.rest_ref, f32[1024,1024]{1,0:T(8,128)} %data_ref.1), custom_call_target="tpu_custom_call" | custom-call | tf_op jit(solution)/shard_map/finish/pallas_call | solution.py:432
Async XLA Ops:
  1.9 1.0 %copy-start = (bf16[1024,256]{1,0:T(8,128)(2,1)S(1)}, bf16[1024,256]{1,0:T(8,128)(2,1)}, u32[]{:S(2)}) copy-start(bf16[1024,256]{1,0:T(8,128)(2,1)} %omega_hbm.1) | copy-start | bytes 1572868
